TPU v7x, 32 devices: a whole 2x2x4 slice. The times are simulated.
32 devices in a mesh: groups: 2 (over y), row: 4 (over z), col: 2 (over x), segment: 2 (over core).
Axes of the slice: x: 2, y: 2, z: 4, core: 2. Of those that a mesh axis runs over, the one named last changes fastest.
Arguments:
- latents: bfloat16 [4, 512, 3072], P(None, ('groups', 'col'), 'row'), parts along dimension 1, may hold values from -6 to 6
- w_in: bfloat16 [2, 3072, 12288], P('segment', 'col', 'row'), may hold values from -0.109375 to 0.109375
- b_in: float32 [2, 12288], P('segment', 'row'), may hold values from -4 to 4
- w_out: bfloat16 [2, 12288, 3072], P('segment', 'row', 'col'), may hold values from -0.0546875 to 0.0546875
- b_out: float32 [2, 3072], P('segment', 'row'), may hold values from -3 to 3
- modulation: float32 [2, 8, 3, 3072], P('segment', 'groups'), parts along dimension 1, may hold values from -3 to 3
Outputs:
- layer_outputs: bfloat16 [2, 4, 512, 3072], P('segment', None, ('groups', 'col'), 'row'), parts along dimension 2
There are 2 independent parts, one for each index of `groups`. A program takes and returns all parts, laid end to end along the dimension named above; an argument that names none is the same for every part. Nothing has to cross between parts.
All inputs are finite; a program needn't handle non-finite values.
Results may differ from a plain program's by a relative error of at most 0.009.
Values may be sent and summed in bfloat16 or wider, within the bound.
A program may use at most 128 MiB of HBM per device.

v0:
```python
import jax
import jax.numpy as jnp
from jax import lax
from jax.sharding import PartitionSpec as P


def shifted(block, axis, distance):
    devices = range(lax.axis_size(axis))
    route = [(i - distance, i) for i in devices if i - distance in devices]
    return lax.ppermute(block, axis, route)


def on_device(latents, w_in, b_in, w_out, b_out, modulation):
    panels = (
        lax.all_gather(w_in, "col", axis=1, tiled=True),
        lax.all_gather(w_out, "col", axis=2, tiled=True),
    )
    w_first = panels[0][0]
    w_second = panels[1][0]
    micro_count = latents.shape[0]
    width = latents.shape[2]
    segment = lax.axis_index("segment")
    segments = lax.axis_size("segment")
    ticks = micro_count + segments - 1
    row_start = lax.axis_index("row") * width
    conditioning = modulation[0]
    bias_first = b_in[0]
    bias_local = b_out[0]
    results = []
    handed = jnp.zeros_like(latents[0])
    for tick in range(ticks):
        if tick > 0:
            handed = shifted(results[-1], "segment", 1)
        first_feed = latents[min(tick, micro_count - 1)]
        feed = jnp.where(segment == 0, first_feed, handed)
        micro = jnp.clip(tick - segment, 0, micro_count - 1)
        mods = lax.dynamic_index_in_dim(conditioning, micro, 0, keepdims=False)
        values = feed.astype(jnp.float32)
        whole = lax.all_gather(feed, "row", axis=1, tiled=True).astype(jnp.float32)
        mean = jnp.mean(whole, axis=-1, keepdims=True)
        var = jnp.mean((whole - mean) ** 2, axis=-1, keepdims=True)
        normed = (whole - mean) * lax.rsqrt(var + 1e-06)
        modulated = (normed * (1.0 + mods[1]) + mods[0]).astype(jnp.bfloat16)
        pre = jnp.dot(modulated, w_first, preferred_element_type=jnp.float32)
        hidden = jax.nn.gelu(pre + bias_first, approximate=True).astype(jnp.bfloat16)
        term = jnp.dot(hidden, w_second, preferred_element_type=jnp.float32)
        branch = lax.psum_scatter(
            term.astype(jnp.bfloat16), "row", scatter_dimension=1, tiled=True
        ).astype(jnp.float32)
        gate_local = lax.dynamic_slice_in_dim(mods[2], row_start, width, 0)
        results.append((values + gate_local * (branch + bias_local)).astype(jnp.bfloat16))
    stacked = jnp.stack(results)
    chosen = lax.dynamic_slice_in_dim(stacked, segment, micro_count, 0)
    return chosen[None]


def solution(mesh):
    return jax.shard_map(
        on_device,
        mesh=mesh,
        in_specs=(
            P(None, ("groups", "col"), "row"),
            P("segment", "col", "row"),
            P("segment", "row"),
            P("segment", "row", "col"),
            P("segment", "row"),
            P("segment", "groups", None, None),
        ),
        out_specs=P("segment", None, ("groups", "col"), "row"),
        check_vma=False,
    )
```

profile of v0, /device:TPU:0, one launch (start us, length us, event | category | flops | bytes accessed | tf_op | source)
XLA Modules:
  0.0 767.9 jit_solution(15648472256520840852)
XLA Ops:
  6.5 0.7 all-gather.4.cloned.1.call-update
  7.3 0.7 all-gather.6.cloned.1.call-update
  8.1 0.3 copy-done
  8.4 21.3 %all-gather = bf16[1,128,3072]{2,1,0:T(8,128)(2,1)S(1)} all-gather(bf16[1,128,768]{2,1,0:T(8,128)(2,1)S(1)} %slice_select_fusion), channel_id=2, replica_groups=mesh['groups'=2,'row'=4,'col'=2,'segment'=2] {'row'}, dimensions={2}, use_global_device_ids=true | all-gather | bytes 983040 | tf_op jit(solution)/shard_map/all_gather | solution.py:39
  29.7 0.2 convert_reduce_fusion
  29.9 0.4 fusion.77
  30.3 0.1 dynamic-slice_add_fusion
  30.4 205.6 %all-gather.4.cloned.1.call-done = bf16[1,3072,3072]{2,1,0:T(8,128)(2,1)} async-done(((bf16[1,1536,3072]{2,1,0:T(8,128)(2,1)}), bf16[1,3072,3072]{2,1,0:T(8,128)(2,1)}) %all-gather.4.cloned.1.call-update) | async-done | bytes 18874384 | tf_op jit(solution)/shard_map/all_gather | solution.py:15
  236.0 225.9 %all-gather.6.cloned.1.call-done = bf16[1,3072,3072]{2,1,0:T(8,128)(2,1)} async-done(((bf16[1,3072,1536]{2,1,0:T(8,128)(2,1)}), bf16[1,3072,3072]{2,1,0:T(8,128)(2,1)}) %all-gather.6.cloned.1.call-update) | async-done | bytes 18874384 | tf_op jit(solution)/shard_map/all_gather | solution.py:16
  461.9 18.4 %fusion.35 = bf16[128,3072]{1,0:T(8,128)(2,1)} fusion(bf16[1,3072,3072]{2,1,0:T(8,128)(2,1)} %all-gather.6.cloned.1.call-done, bf16[1,3072,3072]{2,1,0:T(8,128)(2,1)} %all-gather.4.cloned.1.call-done, bf16[1,128,3072]{2,1,0:T(8,128)(2,1)S(1)} %all-gather, f32[3072]{0:T(1024)S(1)} %bitcast.137, f32[3072]{0:T(1024)S(1)} %bitcast.136, f32[3072]{0:T(1024)S(1)} %bitcast.135, ...), kind=kOutput, calls=%fused_computation.25 | convolution fusion | flops 4838522880 | bytes 39359488 | tf_op jit(solution)/shard_map/dot_general | solution.py:46
  480.4 0.0 reduce-scatter.8.cloned.1.call-start
  480.4 0.1 fusion.193
  480.6 23.2 %reduce-scatter.6.cloned.1.call-done = bf16[128,768]{1,0:T(8,128)(2,1)} async-done(((bf16[128,3072]{1,0:T(8,128)(2,1)}), bf16[128,768]{1,0:T(8,128)(2,1)}) %reduce-scatter.6.cloned.1.call-update) | async-done | bytes 196624 | tf_op jit(solution)/shard_map/reduce_scatter | solution.py:47
  503.8 1.0 bitcast_dynamic-update-slice_fusion.3
  504.8 1.3 collective-permute-start
  506.1 1.0 collective-permute-done
  507.2 18.2 %all_gather.24 = bf16[128,3072]{1,0:T(8,128)(2,1)S(1)} all-gather(bf16[128,768]{1,0:T(8,128)(2,1)S(1)} %bitcast_select_fusion.3), channel_id=1, replica_groups=mesh['groups'=2,'row'=4,'col'=2,'segment'=2] {'row'}, dimensions={1}, use_global_device_ids=true | all-gather | bytes 983040 | tf_op jit(solution)/shard_map/all_gather | solution.py:39
  525.4 0.2 convert_reduce_fusion.4
  525.6 0.4 fusion.70
  526.0 18.4 %fusion.38 = bf16[128,3072]{1,0:T(8,128)(2,1)} fusion(bf16[1,3072,3072]{2,1,0:T(8,128)(2,1)} %all-gather.6.cloned.1.call-done, bf16[1,3072,3072]{2,1,0:T(8,128)(2,1)} %all-gather.4.cloned.1.call-done, bf16[128,3072]{1,0:T(8,128)(2,1)S(1)} %all_gather.24, f32[3072]{0:T(1024)S(1)} %bitcast.134, f32[3072]{0:T(1024)S(1)} %bitcast.133, ...), kind=kOutput, calls=%fused_computation.26 | convolution fusion | flops 4838522880 | bytes 39359488 | tf_op jit(solution)/shard_map/dot_general | solution.py:46
  544.5 23.1 %reduce-scatter.8.cloned.1.call-done = bf16[128,768]{1,0:T(8,128)(2,1)} async-done(((bf16[128,3072]{1,0:T(8,128)(2,1)}), bf16[128,768]{1,0:T(8,128)(2,1)}) %reduce-scatter.8.cloned.1.call-update) | async-done | bytes 196624 | tf_op jit(solution)/shard_map/reduce_scatter | solution.py:47
  567.6 1.0 bitcast_dynamic-update-slice_fusion.2
  568.6 1.3 collective-permute-start.1
  569.9 1.0 collective-permute-done.1
  571.0 18.3 %all_gather.25 = bf16[128,3072]{1,0:T(8,128)(2,1)S(1)} all-gather(bf16[128,768]{1,0:T(8,128)(2,1)S(1)} %bitcast_select_fusion.2), channel_id=1, replica_groups=mesh['groups'=2,'row'=4,'col'=2,'segment'=2] {'row'}, dimensions={1}, use_global_device_ids=true | all-gather | bytes 983040 | tf_op jit(solution)/shard_map/all_gather | solution.py:39
  589.2 0.2 convert_reduce_fusion.3
  589.4 0.4 fusion.66
  589.8 18.4 %fusion.41 = bf16[128,3072]{1,0:T(8,128)(2,1)} fusion(bf16[1,3072,3072]{2,1,0:T(8,128)(2,1)} %all-gather.6.cloned.1.call-done, bf16[1,3072,3072]{2,1,0:T(8,128)(2,1)} %all-gather.4.cloned.1.call-done, bf16[128,3072]{1,0:T(8,128)(2,1)S(1)} %all_gather.25, f32[3072]{0:T(1024)S(1)} %bitcast.132, f32[3072]{0:T(1024)S(1)} %bitcast.131, ...), kind=kOutput, calls=%fused_computation.27 | convolution fusion | flops 4838522880 | bytes 39359488 | tf_op jit(solution)/shard_map/dot_general | solution.py:46
  608.3 0.0 reduce-scatter.12.cloned.1.call-start
  608.3 23.2 %reduce-scatter.10.cloned.1.call-done = bf16[128,768]{1,0:T(8,128)(2,1)} async-done(((bf16[128,3072]{1,0:T(8,128)(2,1)}), bf16[128,768]{1,0:T(8,128)(2,1)}) %reduce-scatter.10.cloned.1.call-update) | async-done | bytes 196624 | tf_op jit(solution)/shard_map/reduce_scatter | solution.py:47
  631.5 1.0 bitcast_dynamic-update-slice_fusion.1
  632.5 1.3 collective-permute-start.2
  633.8 1.0 collective-permute-done.2
  634.9 18.3 %all_gather.26 = bf16[128,3072]{1,0:T(8,128)(2,1)S(1)} all-gather(bf16[128,768]{1,0:T(8,128)(2,1)S(1)} %bitcast_select_fusion.1), channel_id=1, replica_groups=mesh['groups'=2,'row'=4,'col'=2,'segment'=2] {'row'}, dimensions={1}, use_global_device_ids=true | all-gather | bytes 983040 | tf_op jit(solution)/shard_map/all_gather | solution.py:39
  653.2 0.2 convert_reduce_fusion.2
  653.4 0.4 fusion.62
  653.8 18.4 %fusion.44 = bf16[128,3072]{1,0:T(8,128)(2,1)} fusion(bf16[1,3072,3072]{2,1,0:T(8,128)(2,1)} %all-gather.6.cloned.1.call-done, bf16[1,3072,3072]{2,1,0:T(8,128)(2,1)} %all-gather.4.cloned.1.call-done, bf16[128,3072]{1,0:T(8,128)(2,1)S(1)} %all_gather.26, f32[3072]{0:T(1024)S(1)} %bitcast.130, f32[3072]{0:T(1024)S(1)} %bitcast.129, ...), kind=kOutput, calls=%fused_computation.28 | convolution fusion | flops 4838522880 | bytes 39359488 | tf_op jit(solution)/shard_map/dot_general | solution.py:46
  672.3 23.0 %reduce-scatter.12.cloned.1.call-done = bf16[128,768]{1,0:T(8,128)(2,1)} async-done(((bf16[128,3072]{1,0:T(8,128)(2,1)}), bf16[128,768]{1,0:T(8,128)(2,1)}) %reduce-scatter.12.cloned.1.call-update) | async-done | bytes 196624 | tf_op jit(solution)/shard_map/reduce_scatter | solution.py:47
  695.2 1.0 bitcast_dynamic-update-slice_fusion
  696.3 1.3 collective-permute-start.3
  697.6 1.0 collective-permute-done.3
  698.6 18.4 %all_gather.27 = bf16[128,3072]{1,0:T(8,128)(2,1)S(1)} all-gather(bf16[128,768]{1,0:T(8,128)(2,1)S(1)} %bitcast_select_fusion), channel_id=1, replica_groups=mesh['groups'=2,'row'=4,'col'=2,'segment'=2] {'row'}, dimensions={1}, use_global_device_ids=true | all-gather | bytes 983040 | tf_op jit(solution)/shard_map/all_gather | solution.py:39
  717.0 0.2 convert_reduce_fusion.1
  717.2 0.4 fusion.58
  717.6 18.4 %fusion.47 = bf16[128,3072]{1,0:T(8,128)(2,1)} fusion(bf16[1,3072,3072]{2,1,0:T(8,128)(2,1)} %all-gather.6.cloned.1.call-done, bf16[1,3072,3072]{2,1,0:T(8,128)(2,1)} %all-gather.4.cloned.1.call-done, bf16[128,3072]{1,0:T(8,128)(2,1)S(1)} %all_gather.27, f32[3072]{0:T(1024)S(1)} %bitcast.128, f32[3072]{0:T(1024)S(1)} %bitcast.127, ...), kind=kOutput, calls=%fused_computation.29 | convolution fusion | flops 4838522880 | bytes 39359488 | tf_op jit(solution)/shard_map/dot_general | solution.py:46
  736.0 23.0 %reduce-scatter.14.cloned.1.call-done = bf16[128,768]{1,0:T(8,128)(2,1)} async-done(((bf16[128,3072]{1,0:T(8,128)(2,1)}), bf16[128,768]{1,0:T(8,128)(2,1)}) %reduce-scatter.14.cloned.1.call-update) | async-done | bytes 196624 | tf_op jit(solution)/shard_map/reduce_scatter | solution.py:47
  759.1 1.0 fusion.188
  760.1 0.9 dynamic-slice_bitcast_fusion
  (33 shorter events, 0.5 us)
Async XLA Ops:
  6.5 229.5 %all-gather.4.cloned.1.call-start = ((), (), s32[]{:S(2)}) async-start(), calls=%async_computation.5 | async-start | bytes 28311552 | tf_op jit(solution)/shard_map/all_gather | solution.py:15
  7.3 1.1 copy-start
  7.3 454.7 %all-gather.6.cloned.1.call-start = ((), (), s32[]{:S(2)}) async-start(), calls=%async_computation.6 | async-start | bytes 28311552 | tf_op jit(solution)/shard_map/all_gather | solution.py:16
  8.0 22.3 %copy-start.1 = (f32[1,4,3,3072]{3,1,2,0:T(4,128)S(1)}, f32[1,4,3,3072]{3,1,2,0:T(4,128)}, u32[]{:S(2)}) copy-start(f32[1,4,3,3072]{3,1,2,0:T(4,128)} %param.11) | copy-start | bytes 442372
  8.0 495.8 %reduce-scatter.6.cloned.1.call-start = ((), (), s32[]{:S(2)}) async-start(), calls=%async_computation.7 | async-start | bytes 983040 | tf_op jit(solution)/shard_map/reduce_scatter | solution.py:47
  8.4 453.5 %copy-start.3 = (f32[1,3072]{1,0:T(1,128)S(1)}, f32[1,3072]{1,0:T(1,128)}, u32[]{:S(2)}) copy-start(f32[1,3072]{1,0:T(1,128)} %param.8) | copy-start | bytes 36868
  461.9 18.5 %copy-start.2 = (f32[1,768]{1,0:T(1,128)S(1)}, f32[1,768]{1,0:T(1,128)}, u32[]{:S(2)}) copy-start(f32[1,768]{1,0:T(1,128)} %param.10) | copy-start | bytes 9220
  480.4 87.2 %reduce-scatter.8.cloned.1.call-start = ((), (), s32[]{:S(2)}) async-start(), calls=%async_computation.8 | async-start | bytes 983040 | tf_op jit(solution)/shard_map/reduce_scatter | solution.py:47
  504.8 2.4 collective-permute-start
  544.4 87.0 %reduce-scatter.10.cloned.1.call-start = ((), (), s32[]{:S(2)}) async-start(), calls=%async_computation.9 | async-start | bytes 983040 | tf_op jit(solution)/shard_map/reduce_scatter | solution.py:47
  568.6 2.4 collective-permute-start.1
  608.3 87.0 %reduce-scatter.12.cloned.1.call-start = ((), (), s32[]{:S(2)}) async-start(), calls=%async_computation.10 | async-start | bytes 983040 | tf_op jit(solution)/shard_map/reduce_scatter | solution.py:47
  632.5 2.4 collective-permute-start.2
  672.2 86.8 %reduce-scatter.14.cloned.1.call-start = ((), (), s32[]{:S(2)}) async-start(), calls=%async_computation.11 | async-start | bytes 983040 | tf_op jit(solution)/shard_map/reduce_scatter | solution.py:47
  696.3 2.4 collective-permute-start.3
Sparse Core Ops, SparseCore 0:
  8.9 227.0 all-gather.3
  237.6 224.3 all-gather.5
  480.5 23.2 reduce-scatter.5
  544.6 22.9 reduce-scatter.7
  608.4 23.0 reduce-scatter.9
  672.3 22.8 reduce-scatter.11
  736.2 22.8 reduce-scatter.13
where the time goes:
time: 768 us
  waiting for transfers between devices  553 us (72%)
  blocking collectives  94.5 us (12%)
  matrix products  92.1 us (12%)
  between operations  13.6 us (2%)
  other arithmetic  8.14 us (1%)
    all_gather x1, waiting for transfers between devices, on_device(): lax.all_gather(w_out, 'col', axis=2, tiled=True)  226 us
    all_gather x1, waiting for transfers between devices, on_device(): lax.all_gather(w_in, 'col', axis=1, tiled=True)  206 us
    reduce_scatter x5, waiting for transfers between devices, on_device(): lax.psum_scatter(term.astype(jnp.bfloat16), 'row', scatter_dimension=1, t...  115 us
    all_gather x5, blocking collectives, on_device(): whole = lax.all_gather(feed, 'row', axis=1, tiled=True).astype(jnp.float32)  94.5 us
    dot_general x5, matrix products, on_device(): term = jnp.dot(hidden, w_second, preferred_element_type=jnp.float32)  92.1 us
  transfers between devices with their start and end apart: 11, of which 11 were waited for; matrix products, arithmetic and copies ran while one was open for 0% of the time, Pallas kernels for 0%

commit v1 on v0

--- a/solution.py
+++ b/solution.py
@@ -2,6 +2,28 @@
 import jax.numpy as jnp
 from jax import lax
 from jax.sharding import PartitionSpec as P
+
+
+def in_order(parts, dim):
+    shape = list(parts.shape[1:])
+    shape[dim] *= parts.shape[0]
+    return jnp.moveaxis(parts, 0, dim).reshape(shape)
+
+
+def grow_blocks(array, axis):
+    devices = lax.axis_size(axis)
+    pieces = array[None]
+    for level in range(devices.bit_length() - 1):
+        apart = 1 << level
+        received = lax.ppermute(pieces, axis, [(i, i ^ apart) for i in range(devices)])
+        both = jnp.stack([pieces, received])
+        upper = lax.axis_index(axis) >> level & 1
+        pieces = jnp.where(upper == 0, both, both[::-1]).reshape(-1, *array.shape)
+    return pieces
+
+
+def gather_by_bits(value, axis, dim):
+    return in_order(grow_blocks(value, axis), dim)
 
 
 def shifted(block, axis, distance):
@@ -11,10 +33,7 @@
 
 
 def on_device(latents, w_in, b_in, w_out, b_out, modulation):
-    panels = (
-        lax.all_gather(w_in, "col", axis=1, tiled=True),
-        lax.all_gather(w_out, "col", axis=2, tiled=True),
-    )
+    panels = (gather_by_bits(w_in, "col", 1), lax.all_gather(w_out, "col", axis=2, tiled=True))
     w_first = panels[0][0]
     w_second = panels[1][0]
     micro_count = latents.shape[0]

time: 768 us -> 724 us (0.943)
  waiting for transfers between devices: 553 us -> 488 us
  other arithmetic: 8.14 us -> 27.1 us
    ppermute x0 -> x1, waiting for transfers between devices: none -> 364 us  [grow_blocks(): lax.ppermute(pieces, axis, [(i, i ^ apart) for i in range(devices)])]
    all_gather x1, waiting for transfers between devices: 226 us -> 1.76 us  [on_device(): lax.all_gather(w_out, 'col', axis=2, tiled=True)]
    all_gather x1 -> x0, waiting for transfers between devices: 206 us -> none  [on_device(): lax.all_gather(w_in, 'col', axis=1, tiled=True)]
    select_n x0 -> x1, other arithmetic: none -> 9.75 us  [grow_blocks(): pieces = jnp.where(upper == 0, both, both[::-1]).reshape(-1, *array.shape)]
    another operation x0 -> x1, other arithmetic: none -> 9.19 us  [grow_blocks(): both = jnp.stack([pieces, received])]
  transfers between devices with their start and end apart: 11 -> 11, of which waited for: 11 -> 11; matrix products, arithmetic and copies ran while one was open for 0% -> 3% of each run, Pallas kernels for 0% -> 0%
where the time goes in v1:
time: 724 us; the launch traced here: 723 us
  waiting for transfers between devices  488 us (67%)
  blocking collectives  93.2 us (13%)
  matrix products  92.1 us (13%)
  other arithmetic  27.1 us (4%)
  between operations  13.6 us (2%)
  starting transfers between devices  8.42 us (1%)
    ppermute x1, waiting for transfers between devices, grow_blocks(): lax.ppermute(pieces, axis, [(i, i ^ apart) for i in range(devices)])  364 us
    reduce_scatter x5, waiting for transfers between devices, on_device(): lax.psum_scatter(term.astype(jnp.bfloat16), 'row', scatter_dimension=1, t...  117 us
    all_gather x5, blocking collectives, on_device(): whole = lax.all_gather(feed, 'row', axis=1, tiled=True).astype(jnp.float32)  93.2 us
    dot_general x5, matrix products, on_device(): term = jnp.dot(hidden, w_second, preferred_element_type=jnp.float32)  92.1 us
  transfers between devices with their start and end apart: 11, of which 11 were waited for; matrix products, arithmetic and copies ran while one was open for 3% of the time, Pallas kernels for 0%

profile of v1, /device:TPU:0, one launch (start us, length us, event | category | flops | bytes accessed | tf_op | source)
XLA Modules:
  0.0 723.3 jit_solution(3159794816178448700)
XLA Ops:
  6.5 0.7 all-gather.3.cloned.1.call-update
  7.3 3.0 collective-permute-start
  10.3 19.9 %all-gather = bf16[1,128,3072]{2,1,0:T(8,128)(2,1)S(1)} all-gather(bf16[1,128,768]{2,1,0:T(8,128)(2,1)S(1)} %slice_select_fusion), channel_id=2, replica_groups=mesh['groups'=2,'row'=4,'col'=2,'segment'=2] {'row'}, dimensions={2}, use_global_device_ids=true | all-gather | bytes 983040 | tf_op jit(solution)/shard_map/all_gather | solution.py:58
  30.3 0.2 convert_reduce_fusion
  30.5 0.4 fusion.52
  30.8 0.1 dynamic-slice_add_fusion
  31.0 364.2 %collective-permute-done = bf16[1,1,1536,3072]{3,2,1,0:T(8,128)(2,1)} collective-permute-done((bf16[1,1,1536,3072]{3,2,1,0:T(8,128)(2,1)}, bf16[1,1,1536,3072]{3,2,1,0:T(8,128)(2,1)}, u32[]{:S(2)}, u32[]{:S(2)}) %collective-permute-start) | collective-permute-done | bytes 9437216 | tf_op jit(solution)/shard_map/ppermute | solution.py:18
  395.2 9.2 %pad_maximum_fusion = bf16[2,1,1,1536,3072]{4,3,2,1,0:T(8,128)(2,1)S(1)} fusion(bf16[1,1,1,1536,3072]{4,3,2,1,0:T(8,128)(2,1)} %bitcast.6, bf16[1,1,1,1536,3072]{4,3,2,1,0:T(8,128)(2,1)} %bitcast.91), kind=kLoop, calls=%fused_computation.1 | loop fusion | flops 9437184 | bytes 37748736 | tf_op jit(solution)/shard_map/stack | solution.py:19
  404.4 9.7 %reverse_select_fusion = bf16[2,1,1,1536,3072]{4,3,2,1,0:T(8,128)(2,1)} fusion(bf16[2,1,1,1536,3072]{4,3,2,1,0:T(8,128)(2,1)S(1)} %pad_maximum_fusion, pred[]{:T(512)S(6)} %eq.5), kind=kLoop, calls=%fused_computation | loop fusion | flops 9437184 | bytes 37748736 | tf_op jit(solution)/shard_map/jit(_where)/select_n | solution.py:21
  414.2 1.8 all-gather.3.cloned.1.call-done
  415.9 18.4 %fusion.10 = bf16[128,3072]{1,0:T(8,128)(2,1)} fusion(bf16[1,3072,3072]{2,1,0:T(8,128)(2,1)} %all-gather.3.cloned.1.call-done, bf16[3072,3072]{1,0:T(8,128)(2,1)} %bitcast.85, bf16[1,128,3072]{2,1,0:T(8,128)(2,1)S(1)} %all-gather, f32[3072]{0:T(1024)S(1)} %bitcast.102, f32[3072]{0:T(1024)S(1)} %bitcast.101, f32[3072]{0:T(1024)S(1)} %bitcast.100, ...), kind=kOutput, calls=%fused_computation.17 | convolution fusion | flops 4838522880 | bytes 39359488 | tf_op jit(solution)/shard_map/dot_general | solution.py:65
  434.4 0.0 reduce-scatter.8.cloned.1.call-start
  434.5 0.1 fusion.138
  434.6 24.7 %reduce-scatter.6.cloned.1.call-done = bf16[128,768]{1,0:T(8,128)(2,1)} async-done(((bf16[128,3072]{1,0:T(8,128)(2,1)}), bf16[128,768]{1,0:T(8,128)(2,1)}) %reduce-scatter.6.cloned.1.call-update) | async-done | bytes 196624 | tf_op jit(solution)/shard_map/reduce_scatter | solution.py:66
  459.3 1.0 bitcast_dynamic-update-slice_fusion.3
  460.3 1.3 collective-permute-start.1
  461.6 1.0 collective-permute-done.1
  462.7 18.3 %all_gather.20 = bf16[128,3072]{1,0:T(8,128)(2,1)S(1)} all-gather(bf16[128,768]{1,0:T(8,128)(2,1)S(1)} %bitcast_select_fusion.3), channel_id=1, replica_groups=mesh['groups'=2,'row'=4,'col'=2,'segment'=2] {'row'}, dimensions={1}, use_global_device_ids=true | all-gather | bytes 983040 | tf_op jit(solution)/shard_map/all_gather | solution.py:58
  481.0 0.2 convert_reduce_fusion.4
  481.2 0.4 fusion.45
  481.6 18.4 %fusion.13 = bf16[128,3072]{1,0:T(8,128)(2,1)} fusion(bf16[1,3072,3072]{2,1,0:T(8,128)(2,1)} %all-gather.3.cloned.1.call-done, bf16[3072,3072]{1,0:T(8,128)(2,1)} %bitcast.86, bf16[128,3072]{1,0:T(8,128)(2,1)S(1)} %all_gather.20, f32[3072]{0:T(1024)S(1)} %bitcast.99, f32[3072]{0:T(1024)S(1)} %bitcast.98, f32[128]{0:T(128)S(1)} %add_rsqrt_fusion.3, ...), kind=kOutput, calls=%fused_computation.18 | convolution fusion | flops 4838522880 | bytes 39359488 | tf_op jit(solution)/shard_map/dot_general | solution.py:65
  500.1 23.1 %reduce-scatter.8.cloned.1.call-done = bf16[128,768]{1,0:T(8,128)(2,1)} async-done(((bf16[128,3072]{1,0:T(8,128)(2,1)}), bf16[128,768]{1,0:T(8,128)(2,1)}) %reduce-scatter.8.cloned.1.call-update) | async-done | bytes 196624 | tf_op jit(solution)/shard_map/reduce_scatter | solution.py:66
  523.2 1.0 bitcast_dynamic-update-slice_fusion.2
  524.2 1.3 collective-permute-start.2
  525.5 1.0 collective-permute-done.2
  526.5 18.3 %all_gather.21 = bf16[128,3072]{1,0:T(8,128)(2,1)S(1)} all-gather(bf16[128,768]{1,0:T(8,128)(2,1)S(1)} %bitcast_select_fusion.2), channel_id=1, replica_groups=mesh['groups'=2,'row'=4,'col'=2,'segment'=2] {'row'}, dimensions={1}, use_global_device_ids=true | all-gather | bytes 983040 | tf_op jit(solution)/shard_map/all_gather | solution.py:58
  544.9 0.2 convert_reduce_fusion.3
  545.1 0.4 fusion.41
  545.4 18.4 %fusion.16 = bf16[128,3072]{1,0:T(8,128)(2,1)} fusion(bf16[1,3072,3072]{2,1,0:T(8,128)(2,1)} %all-gather.3.cloned.1.call-done, bf16[3072,3072]{1,0:T(8,128)(2,1)} %bitcast.87, bf16[128,3072]{1,0:T(8,128)(2,1)S(1)} %all_gather.21, f32[3072]{0:T(1024)S(1)} %bitcast.97, f32[3072]{0:T(1024)S(1)} %bitcast.96, f32[128]{0:T(128)S(1)} %add_rsqrt_fusion.2, ...), kind=kOutput, calls=%fused_computation.19 | convolution fusion | flops 4838522880 | bytes 39359488 | tf_op jit(solution)/shard_map/dot_general | solution.py:65
  564.0 23.0 %reduce-scatter.10.cloned.1.call-done = bf16[128,768]{1,0:T(8,128)(2,1)} async-done(((bf16[128,3072]{1,0:T(8,128)(2,1)}), bf16[128,768]{1,0:T(8,128)(2,1)}) %reduce-scatter.10.cloned.1.call-update) | async-done | bytes 196624 | tf_op jit(solution)/shard_map/reduce_scatter | solution.py:66
  587.0 1.0 bitcast_dynamic-update-slice_fusion.1
  588.0 1.3 collective-permute-start.3
  589.3 1.0 collective-permute-done.3
  590.3 18.3 %all_gather.22 = bf16[128,3072]{1,0:T(8,128)(2,1)S(1)} all-gather(bf16[128,768]{1,0:T(8,128)(2,1)S(1)} %bitcast_select_fusion.1), channel_id=1, replica_groups=mesh['groups'=2,'row'=4,'col'=2,'segment'=2] {'row'}, dimensions={1}, use_global_device_ids=true | all-gather | bytes 983040 | tf_op jit(solution)/shard_map/all_gather | solution.py:58
  608.6 0.2 convert_reduce_fusion.2
  608.8 0.4 fusion.37
  609.2 18.4 %fusion.19 = bf16[128,3072]{1,0:T(8,128)(2,1)} fusion(bf16[1,3072,3072]{2,1,0:T(8,128)(2,1)} %all-gather.3.cloned.1.call-done, bf16[3072,3072]{1,0:T(8,128)(2,1)} %bitcast.88, bf16[128,3072]{1,0:T(8,128)(2,1)S(1)} %all_gather.22, f32[3072]{0:T(1024)S(1)} %bitcast.95, f32[3072]{0:T(1024)S(1)} %bitcast.94, f32[128]{0:T(128)S(1)} %add_rsqrt_fusion.1, ...), kind=kOutput, calls=%fused_computation.20 | convolution fusion | flops 4838522880 | bytes 39359488 | tf_op jit(solution)/shard_map/dot_general | solution.py:65
  627.7 23.0 %reduce-scatter.12.cloned.1.call-done = bf16[128,768]{1,0:T(8,128)(2,1)} async-done(((bf16[128,3072]{1,0:T(8,128)(2,1)}), bf16[128,768]{1,0:T(8,128)(2,1)}) %reduce-scatter.12.cloned.1.call-update) | async-done | bytes 196624 | tf_op jit(solution)/shard_map/reduce_scatter | solution.py:66
  650.7 1.0 bitcast_dynamic-update-slice_fusion
  651.7 1.3 collective-permute-start.4
  653.0 1.0 collective-permute-done.4
  654.1 18.4 %all_gather.23 = bf16[128,3072]{1,0:T(8,128)(2,1)S(1)} all-gather(bf16[128,768]{1,0:T(8,128)(2,1)S(1)} %bitcast_select_fusion), channel_id=1, replica_groups=mesh['groups'=2,'row'=4,'col'=2,'segment'=2] {'row'}, dimensions={1}, use_global_device_ids=true | all-gather | bytes 983040 | tf_op jit(solution)/shard_map/all_gather | solution.py:58
  672.5 0.2 convert_reduce_fusion.1
  672.7 0.4 fusion.33
  673.0 18.4 %fusion.22 = bf16[128,3072]{1,0:T(8,128)(2,1)} fusion(bf16[1,3072,3072]{2,1,0:T(8,128)(2,1)} %all-gather.3.cloned.1.call-done, bf16[3072,3072]{1,0:T(8,128)(2,1)} %bitcast.89, bf16[128,3072]{1,0:T(8,128)(2,1)S(1)} %all_gather.23, f32[3072]{0:T(1024)S(1)} %bitcast.93, f32[3072]{0:T(1024)S(1)} %bitcast.92, f32[128]{0:T(128)S(1)} %add_rsqrt_fusion, ...), kind=kOutput, calls=%fused_computation.21 | convolution fusion | flops 4838522880 | bytes 39359488 | tf_op jit(solution)/shard_map/dot_general | solution.py:65
  691.5 23.1 %reduce-scatter.14.cloned.1.call-done = bf16[128,768]{1,0:T(8,128)(2,1)} async-done(((bf16[128,3072]{1,0:T(8,128)(2,1)}), bf16[128,768]{1,0:T(8,128)(2,1)}) %reduce-scatter.14.cloned.1.call-update) | async-done | bytes 196624 | tf_op jit(solution)/shard_map/reduce_scatter | solution.py:66
  714.5 1.0 fusion.133
  715.5 0.9 dynamic-slice_bitcast_fusion
  (34 shorter events, 0.5 us)
Async XLA Ops:
  6.5 3.8 copy-start
  6.5 409.4 %all-gather.3.cloned.1.call-start = ((), (), s32[]{:S(2)}) async-start(), calls=%async_computation.5 | async-start | bytes 28311552 | tf_op jit(solution)/shard_map/all_gather | solution.py:36
  7.3 23.6 %copy-start.1 = (f32[1,4,3,3072]{3,1,2,0:T(4,128)S(1)}, f32[1,4,3,3072]{3,1,2,0:T(4,128)}, u32[]{:S(2)}) copy-start(f32[1,4,3,3072]{3,1,2,0:T(4,128)} %param.11) | copy-start | bytes 442372
  7.3 452.0 %reduce-scatter.6.cloned.1.call-start = ((), (), s32[]{:S(2)}) async-start(), calls=%async_computation.6 | async-start | bytes 983040 | tf_op jit(solution)/shard_map/reduce_scatter | solution.py:66
  7.3 387.9 %collective-permute-start = (bf16[1,1,1536,3072]{3,2,1,0:T(8,128)(2,1)}, bf16[1,1,1536,3072]{3,2,1,0:T(8,128)(2,1)}, u32[]{:S(2)}, u32[]{:S(2)}) collective-permute-start(bf16[1,1,1536,3072]{3,2,1,0:T(8,128)(2,1)} %bitcast.90), channel_id=1, source_target_pairs={{0,2},{2,0},{1,3},{3,1},{4,6},{6,4},{5,7},{7,5},{8,10},{10,8},{9,1... | collective-permute-start | bytes 28311560 | tf_op jit(solution)/shard_map/ppermute | solution.py:18
  404.4 11.5 %copy-start.3 = (f32[1,3072]{1,0:T(1,128)S(1)}, f32[1,3072]{1,0:T(1,128)}, u32[]{:S(2)}) copy-start(f32[1,3072]{1,0:T(1,128)} %param.8) | copy-start | bytes 36868
  415.9 18.5 %copy-start.2 = (f32[1,768]{1,0:T(1,128)S(1)}, f32[1,768]{1,0:T(1,128)}, u32[]{:S(2)}) copy-start(f32[1,768]{1,0:T(1,128)} %param.10) | copy-start | bytes 9220
  434.4 88.8 %reduce-scatter.8.cloned.1.call-start = ((), (), s32[]{:S(2)}) async-start(), calls=%async_computation.7 | async-start | bytes 983040 | tf_op jit(solution)/shard_map/reduce_scatter | solution.py:66
  460.3 2.4 collective-permute-start.1
  500.0 86.9 %reduce-scatter.10.cloned.1.call-start = ((), (), s32[]{:S(2)}) async-start(), calls=%async_computation.8 | async-start | bytes 983040 | tf_op jit(solution)/shard_map/reduce_scatter | solution.py:66
  524.2 2.4 collective-permute-start.2
  563.9 86.8 %reduce-scatter.12.cloned.1.call-start = ((), (), s32[]{:S(2)}) async-start(), calls=%async_computation.9 | async-start | bytes 983040 | tf_op jit(solution)/shard_map/reduce_scatter | solution.py:66
  588.0 2.4 collective-permute-start.3
  627.7 86.9 %reduce-scatter.14.cloned.1.call-start = ((), (), s32[]{:S(2)}) async-start(), calls=%async_computation.10 | async-start | bytes 983040 | tf_op jit(solution)/shard_map/reduce_scatter | solution.py:66
  651.7 2.4 collective-permute-start.4
Sparse Core Ops, SparseCore 0:
  8.9 406.9 all-gather.2
  434.5 24.7 reduce-scatter.5
  500.1 22.9 reduce-scatter.7
  564.0 22.8 reduce-scatter.9
  627.8 22.8 reduce-scatter.11
  691.6 22.8 reduce-scatter.13
